TPU v7x, 1024 devices: a whole 4x8x16 slice. The times are simulated.
1024 devices in a mesh: group: 16 (over y, core), dom: 64 (over z, x).
Axes of the slice: x: 4, y: 8, z: 16, core: 2. Of those that a mesh axis runs over, the one named last changes fastest.
Arguments:
- node_state: bfloat16 [524288, 256], P(('group', 'dom')), may hold values from -6 to 6
- cotangent: bfloat16 [524288, 256], P(('group', 'dom')), may hold values from -6 to 6
- stale_domain: bfloat16 [524288, 256], P(('group', 'dom')), may hold values from -6 to 6
- stale_group: bfloat16 [131072, 256], P(('group', 'dom')), may hold values from -6 to 6
- stale_gradient: bfloat16 [524288, 256], P(('group', 'dom')), may hold values from -4 to 4
- tile_values: bfloat16 [32768, 128, 128], P(('group', 'dom')), may hold values from 0 to 0.1, as said below
- tile_source: int32 [32768], P(('group', 'dom')), may hold values from 0 to 8
- tile_target: int32 [32768], P(('group', 'dom')), may hold values from 0 to 3
- tile_count: int32 [1024], P(('group', 'dom')), may hold values from 4 to 32, as said below
- send_domain: int32 [524288], P(('group', 'dom')), may hold values from 0 to 511
- count_domain: int32 [65536], P(('group', 'dom')), may hold values from 1 to 8, as said below
- send_group: int32 [131072], P(('group', 'dom')), may hold values from 0 to 511
- count_group: int32 [16384], P(('group', 'dom')), may hold values from 1 to 8, as said below
- weight_self: bfloat16 [256, 256], replicated, may hold values from -0.375 to 0.375
- weight_neighbour: bfloat16 [256, 256], replicated, may hold values from -0.375 to 0.375
- bias_vector: float32 [256], replicated, may hold values from -4 to 4
Outputs:
- activation: bfloat16 [524288, 256], P(('group', 'dom'))
- state_gradient: bfloat16 [524288, 256], P(('group', 'dom'))
- next_domain: bfloat16 [524288, 256], P(('group', 'dom'))
- next_group: bfloat16 [131072, 256], P(('group', 'dom'))
- next_gradient: bfloat16 [524288, 256], P(('group', 'dom'))
- grad_self: float32 [256, 256], replicated
- grad_neighbour: float32 [256, 256], replicated
- grad_bias: float32 [256], replicated
Inputs may be any that keep to these rules, and one draw needn't show every extreme that they name: `tile_count`: each device's tiles at positions at or above its count are ignored; the counts are 32 divided by 1, 2, 4 or 8, and some device has exactly 32. `count_domain`: counts of live slots toward each partner of the same group; in every group some device receives 8 live rows from every partner. `count_group`: counts of live slots toward each group; for every partition index some device receives 8 live rows from every group. `tile_values`: edge weights, zero for missing edges.
All inputs are finite; a program needn't handle non-finite values.
Results may differ from a plain program's by a relative error of at most 0.0065.
Values may be sent and summed in bfloat16 or wider, within the bound.
No kernel may reach another device: no remote copies, remote signals or barrier semaphores. Data moves between devices by JAX's collectives and lax.ppermute only.
A program may use at most 64 MiB of HBM per device.

v0:
```python
import jax
import jax.numpy as jnp
from jax import lax
from jax.sharding import PartitionSpec as P


def silu_slope(preact):
    sigmoid = jax.nn.sigmoid(preact)
    return sigmoid * (1.0 + preact * (1.0 - sigmoid))


def filled_slots(indices, counts):
    per_peer = indices.shape[0] // counts.shape[0]
    return (jnp.arange(per_peer)[None, :] < counts[:, None]).reshape(-1)


def pack_rows(source, indices, counts):
    filled = filled_slots(indices, counts)
    return jnp.where(
        filled[:, None], jnp.take(source, indices, axis=0), jnp.zeros((), source.dtype)
    )


def spread_rows(totals, arrived, indices, counts):
    filled = filled_slots(indices, counts)
    addend = jnp.where(filled[:, None], arrived.astype(jnp.float32), jnp.zeros((), jnp.float32))
    return totals.at[indices].add(addend)


def local(
    node_state,
    cotangent,
    stale_domain,
    stale_group,
    stale_gradient,
    tile_values,
    tile_source,
    tile_target,
    tile_count,
    send_domain,
    count_domain,
    send_group,
    count_group,
    weight_self,
    weight_neighbour,
    bias_vector,
):
    highest = lax.Precision.HIGHEST
    node_rows, feature_width = node_state.shape
    tile_rows = tile_values.shape[1]
    tile_slots = tile_values.shape[0]
    own_blocks = node_rows // tile_rows
    domain_rows = stale_domain.shape[0]
    outgoing_domain = pack_rows(node_state, send_domain, count_domain)
    next_domain = lax.all_to_all(outgoing_domain, "dom", split_axis=0, concat_axis=0, tiled=True)
    outgoing_group = pack_rows(node_state, send_group, count_group)
    next_group = lax.all_to_all(outgoing_group, "group", split_axis=0, concat_axis=0, tiled=True)
    extended = jnp.concatenate([node_state, stale_domain, stale_group], 0)
    ext_blocks = extended.shape[0] // tile_rows
    blocks = extended.reshape(ext_blocks, tile_rows, feature_width)
    active = jnp.arange(tile_slots) < tile_count[0]
    products = jnp.einsum(
        "kij,kjh->kih",
        tile_values,
        jnp.take(blocks, tile_source, axis=0),
        preferred_element_type=jnp.float32,
    )
    target_hit = (
        (tile_target[None, :] == jnp.arange(own_blocks)[:, None]) & active[None, :]
    ).astype(jnp.float32)
    gathered = (
        jnp.einsum("bk,kih->bih", target_hit, products, precision=highest)
        .reshape(node_rows, feature_width)
        .astype(jnp.bfloat16)
    )
    preact = (
        jnp.dot(node_state, weight_self, preferred_element_type=jnp.float32)
        + jnp.dot(gathered, weight_neighbour, preferred_element_type=jnp.float32)
        + bias_vector
    )
    activation = jax.nn.silu(preact).astype(jnp.bfloat16)
    pre_grad = (cotangent.astype(jnp.float32) * silu_slope(preact)).astype(jnp.bfloat16)
    local_self = jnp.einsum("na,nb->ab", node_state, pre_grad, preferred_element_type=jnp.float32)
    local_neigh = jnp.einsum("na,nb->ab", gathered, pre_grad, preferred_element_type=jnp.float32)
    local_bias = jnp.sum(pre_grad.astype(jnp.float32), 0)
    agg_grad = jnp.einsum(
        "nb,ab->na", pre_grad, weight_neighbour, preferred_element_type=jnp.float32
    ).astype(jnp.bfloat16)
    agg_blocks = agg_grad.reshape(own_blocks, tile_rows, feature_width)
    returned = jnp.einsum(
        "kij,kih->kjh",
        tile_values,
        jnp.take(agg_blocks, tile_target, axis=0),
        preferred_element_type=jnp.float32,
    )
    source_hit = (
        (tile_source[None, :] == jnp.arange(ext_blocks)[:, None]) & active[None, :]
    ).astype(jnp.float32)
    ext_grad = jnp.einsum("ek,kjh->ejh", source_hit, returned, precision=highest).reshape(
        -1, feature_width
    )
    own_term = jnp.einsum("nb,ab->na", pre_grad, weight_self, preferred_element_type=jnp.float32)
    state_gradient = (own_term + ext_grad[:node_rows] + stale_gradient.astype(jnp.float32)).astype(
        jnp.bfloat16
    )
    back_domain = ext_grad[node_rows : node_rows + domain_rows].astype(jnp.bfloat16)
    back_group = ext_grad[node_rows + domain_rows :].astype(jnp.bfloat16)
    arrived_domain = lax.all_to_all(back_domain, "dom", split_axis=0, concat_axis=0, tiled=True)
    arrived_group = lax.all_to_all(back_group, "group", split_axis=0, concat_axis=0, tiled=True)
    totals = jnp.zeros((node_rows, feature_width), jnp.float32)
    totals = spread_rows(totals, arrived_domain, send_domain, count_domain)
    totals = spread_rows(totals, arrived_group, send_group, count_group)
    next_gradient = totals.astype(jnp.bfloat16)
    summed = lax.psum((local_self, local_neigh, local_bias), ("group", "dom"))
    all_nodes = node_rows * lax.axis_size("group") * lax.axis_size("dom")
    grad_self = summed[0] / all_nodes
    grad_neighbour = summed[1] / all_nodes
    grad_bias = summed[2] / all_nodes
    return (
        activation,
        state_gradient,
        next_domain,
        next_group,
        next_gradient,
        grad_self,
        grad_neighbour,
        grad_bias,
    )


def solution(mesh):
    return jax.shard_map(
        local,
        mesh=mesh,
        in_specs=(
            P(("group", "dom"), None),
            P(("group", "dom"), None),
            P(("group", "dom"), None),
            P(("group", "dom"), None),
            P(("group", "dom"), None),
            P(("group", "dom"), None, None),
            P(("group", "dom")),
            P(("group", "dom")),
            P(("group", "dom")),
            P(("group", "dom")),
            P(("group", "dom")),
            P(("group", "dom")),
            P(("group", "dom")),
            P(),
            P(),
            P(),
        ),
        out_specs=(
            P(("group", "dom"), None),
            P(("group", "dom"), None),
            P(("group", "dom"), None),
            P(("group", "dom"), None),
            P(("group", "dom"), None),
            P(),
            P(),
            P(),
        ),
        check_vma=False,
    )
```

profile of v0, /device:TPU:1, one launch (start us, length us, event | category | flops | bytes accessed | tf_op | source)
XLA Modules:
  0.0 605.1 jit_solution(9075535317166244099)
XLA Ops:
  7.2 0.7 compare_select_fusion.1
  7.9 0.7 compare_and_fusion
  8.7 0.7 iota_compare_fusion.1
  9.4 1.7 gather_fusion.3
  11.2 0.7 fusion.24
  11.9 17.4 %all-to-all-start.1 = ((bf16[16,8,256]{2,1,0:T(8,128)(2,1)}), bf16[16,8,256]{2,1,0:T(8,128)(2,1)S(1)}, u32[]{:S(2)}, u32[]{:S(2)}) async-start(bf16[16,8,256]{2,1,0:T(8,128)(2,1)} %fusion.24), calls=%async_computation.1 | async-start | bytes 131072 | tf_op jit(solution)/shard_map/all_to_all | solution.py:57
  29.4 0.7 compare_select_fusion.3
  30.0 0.7 compare_and_fusion.3
  30.7 0.7 compare_select_fusion
  31.4 0.7 compare_and_fusion.1
  32.0 1.2 fusion.40
  33.3 1.1 pad_maximum_fusion
  34.4 2.0 gather_fusion
  36.4 4.4 fusion.6
  40.8 5.5 copy.34
  47.0 3.7 fusion.13
  50.8 1.1 convert_reduce_fusion
  51.9 0.2 convolution_convert_fusion
  52.2 2.0 gather_fusion.2
  54.3 2.0 gather_fusion.1
  56.3 0.9 fusion.18
  57.2 13.1 %all-to-all-start = ((bf16[64,8,256]{2,1,0:T(8,128)(2,1)}), bf16[64,8,256]{2,1,0:T(8,128)(2,1)S(1)}, u32[]{:S(2)}, u32[]{:S(2)}) async-start(bf16[64,8,256]{2,1,0:T(8,128)(2,1)} %fusion.18), calls=%async_computation | async-start | bytes 524288 | tf_op jit(solution)/shard_map/all_to_all | solution.py:55
  70.4 4.4 fusion.4
  74.8 5.5 copy.35
  80.3 5.1 fusion.39
  85.3 0.1 slice.29
  85.5 0.7 copy.30
  86.2 4.7 all-to-all-done
  90.9 9.8 %all-to-all-start.2 = ((bf16[64,8,256]{2,1,0:T(8,128)(2,1)}), bf16[64,8,256]{2,1,0:T(8,128)(2,1)S(1)}, u32[]{:S(2)}, u32[]{:S(2)}) async-start(bf16[64,8,256]{2,1,0:T(8,128)(2,1)} %bitcast.70), calls=%async_computation.2 | async-start | bytes 524288 | tf_op jit(solution)/shard_map/all_to_all | solution.py:108
  100.8 1.0 convolution_bitcast_fusion
  101.8 1.0 fusion.41
  102.8 125.5 %psum.23 = f32[256]{0:T(256)S(1)} all-reduce(f32[256]{0:T(256)S(1)} %get-tuple-element.26), channel_id=1, replica_groups=mesh['group'=16,'dom'=64] {'group','dom'}, use_global_device_ids=true, to_apply=%region_5.6 | all-reduce | flops 256 | bytes 2048 | tf_op jit(solution)/shard_map/psum | solution.py:114
  228.3 0.6 broadcast_multiply_fusion.2
  228.8 0.1 lt.115
  229.1 1.3 slice.28
  230.4 0.1 copy.29
  230.5 0.6 copy.39
  231.2 1.0 fusion.12
  232.1 5.9 all-to-all-start.3
  238.0 349.9 %all-reduce.3.cloned.1.call-done = (f32[256,256]{0,1:T(8,128)}, f32[256,256]{0,1:T(8,128)}) async-done(((f32[256,256]{0,1:T(8,128)}, f32[256,256]{0,1:T(8,128)}), (f32[256,256]{0,1:T(8,128)}, f32[256,256]{0,1:T(8,128)})) %all-reduce.3.cloned.1.call-update) | async-done | bytes 524304 | tf_op jit(solution)/shard_map/psum | solution.py:114
  587.9 1.1 broadcast_multiply_fusion
  589.0 0.8 copy.32
  589.8 0.8 copy.33
  590.6 4.0 scatter_custom_fusion
  594.6 1.6 scatter_custom_fusion.1
  596.2 0.7 convert_element_type.68
  596.9 0.7 copy.46
  597.6 0.6 copy.47
  (40 shorter events, 0.6 us)
Async XLA Ops:
  7.2 29.2 %copy-start = (bf16[32,128,128]{2,1,0:T(8,128)(2,1)S(1)}, bf16[32,128,128]{2,1,0:T(8,128)(2,1)}, u32[]{:S(2)}) copy-start(bf16[32,128,128]{2,1,0:T(8,128)(2,1)} %param.21) | copy-start | bytes 3145732
  11.9 45.3 %all-to-all-start.1 = ((bf16[16,8,256]{2,1,0:T(8,128)(2,1)}), bf16[16,8,256]{2,1,0:T(8,128)(2,1)S(1)}, u32[]{:S(2)}, u32[]{:S(2)}) async-start(bf16[16,8,256]{2,1,0:T(8,128)(2,1)} %fusion.24), calls=%async_computation.1 | async-start | bytes 131072 | tf_op jit(solution)/shard_map/all_to_all | solution.py:57
  40.8 6.2 %copy-start.6 = (s32[32]{0:T(128)S(1)}, s32[32]{0:T(128)}, u32[]{:S(2)}) copy-start(s32[32]{0:T(128)} %param.23) | copy-start | bytes 388
  46.9 3.8 copy-start.5
  46.9 3.8 copy-start.9
  47.0 3.8 copy-start.10
  50.7 1.4 copy-start.1
  51.9 2.4 copy-start.8
  57.2 33.7 %all-to-all-start = ((bf16[64,8,256]{2,1,0:T(8,128)(2,1)}), bf16[64,8,256]{2,1,0:T(8,128)(2,1)S(1)}, u32[]{:S(2)}, u32[]{:S(2)}) async-start(bf16[64,8,256]{2,1,0:T(8,128)(2,1)} %fusion.18), calls=%async_computation | async-start | bytes 524288 | tf_op jit(solution)/shard_map/all_to_all | solution.py:55
  74.8 5.5 copy-start.7
  90.9 141.2 %all-to-all-start.2 = ((bf16[64,8,256]{2,1,0:T(8,128)(2,1)}), bf16[64,8,256]{2,1,0:T(8,128)(2,1)S(1)}, u32[]{:S(2)}, u32[]{:S(2)}) async-start(bf16[64,8,256]{2,1,0:T(8,128)(2,1)} %bitcast.70), calls=%async_computation.2 | async-start | bytes 524288 | tf_op jit(solution)/shard_map/all_to_all | solution.py:108
  100.8 487.1 %all-reduce.3.cloned.1.call-start = ((), (), s32[]{:S(2)}) async-start(), calls=%async_computation.4 | async-start | bytes 1048576 | tf_op jit(solution)/shard_map/psum | solution.py:114
  101.8 129.4 %copy-start.3 = (bf16[256,256]{1,0:T(8,128)(2,1)S(1)}, bf16[256,256]{1,0:T(8,128)(2,1)}, u32[]{:S(2)}) copy-start(bf16[256,256]{1,0:T(8,128)(2,1)} %param.29) | copy-start | bytes 393220
  102.8 128.4 %copy-start.4 = (bf16[512,256]{1,0:T(8,128)(2,1)S(1)}, bf16[512,256]{1,0:T(8,128)(2,1)}, u32[]{:S(2)}) copy-start(bf16[512,256]{1,0:T(8,128)(2,1)} %param.20) | copy-start | bytes 786436
  232.1 358.5 %copy-start.2 = (bf16[64,8,256]{2,1,0:T(8,128)(2,1)}, bf16[64,8,256]{2,1,0:T(8,128)(2,1)S(1)}, u32[]{:S(2)}) copy-start(bf16[64,8,256]{2,1,0:T(8,128)(2,1)S(1)} %all-to-all-done.2) | copy-start | bytes 786436
  232.1 362.5 %all-to-all-start.3 = ((bf16[16,8,256]{2,1,0:T(8,128)(2,1)}), bf16[16,8,256]{2,1,0:T(8,128)(2,1)S(1)}, u32[]{:S(2)}, u32[]{:S(2)}) async-start(bf16[16,8,256]{2,1,0:T(8,128)(2,1)} %bitcast.62), calls=%async_computation.3 | async-start | bytes 131072 | tf_op jit(solution)/shard_map/all_to_all | solution.py:109
Sparse Core Ops, SparseCore 0:
  107.8 480.0 all-reduce.2
where the time goes:
time: 608 us; the launch traced here: 605 us
  waiting for transfers between devices  355 us (58%)
  blocking collectives  125 us (21%)
  starting transfers between devices  46.3 us (8%)
  local copies, waits for them, and re-layouts  25.1 us (4%)
  matrix products  23 us (4%)
  other arithmetic  15.6 us (3%)
  between operations  15 us (2%)
    psum x1, waiting for transfers between devices, local(): summed = lax.psum((local_self, local_neigh, local_bias), ('group', 'dom'))  350 us
    psum x1, blocking collectives, local(): summed = lax.psum((local_self, local_neigh, local_bias), ('group', 'dom'))  125 us
    all_to_all x1, starting transfers between devices, local(): lax.all_to_all(outgoing_group, 'group', split_axis=0, concat_axis=0, tile...  17.4 us
    all_to_all x1, starting transfers between devices, local(): lax.all_to_all(outgoing_domain, 'dom', split_axis=0, concat_axis=0, tiled...  13.1 us
  transfers between devices with their start and end apart: 5, of which 2 were waited for; matrix products, arithmetic and copies ran while one was open for 9% of the time, Pallas kernels for 0%

commit v1 on v0

v1 whole, which is shorter than its diff:
```python
import functools

import jax
import jax.numpy as jnp
from jax import lax
from jax.experimental import pallas as pl
from jax.experimental.pallas import tpu as pltpu
from jax.sharding import Mesh
from jax.sharding import PartitionSpec as P

F32 = jnp.float32
BF16 = jnp.bfloat16
VMEM = pl.BlockSpec(memory_space=pltpu.VMEM)
SMEM = pl.BlockSpec(memory_space=pltpu.SMEM)
UNROLL = 4
EXTRA = 8
X_SIZE = 4
CONTRACT_FIRST = (((0,), (0,)), ((), ()))
CONTRACT_LAST = (((1,), (1,)), ((), ()))


def kernel_params():
    return pltpu.CompilerParams(vmem_limit_bytes=48 * 1024 * 1024)


def dot(left, right):
    return jnp.dot(left, right, preferred_element_type=F32)


def slot_matrix(indices, counts, rows):
    slots = indices.shape[1]
    peers = counts.shape[1]
    per_peer = slots // peers
    peer = lax.broadcasted_iota(jnp.int32, (peers, slots), 0)
    slot = lax.broadcasted_iota(jnp.int32, (peers, slots), 1)
    owner = (slot // per_peer == peer).astype(F32)
    limit = dot(jnp.broadcast_to(counts.astype(F32), (8, peers)), owner)[0:1]
    place = lax.broadcasted_iota(jnp.int32, (1, slots), 1) % per_peer
    named = jnp.where(place.astype(F32) < limit, indices, -1)
    row = lax.broadcasted_iota(jnp.int32, (rows, slots), 0)
    return (row == named).astype(F32).astype(BF16)


def layer_kernel(
    source,
    target,
    count,
    state,
    cotangent,
    stale_domain,
    stale_group,
    stale_gradient,
    tiles,
    send_domain,
    count_domain,
    send_group,
    count_group,
    weight_self,
    weight_neighbour,
    bias,
    activation,
    state_gradient,
    out_domain,
    out_group,
    partial,
    extended,
    gathered,
    agg,
    ext_grad,
):
    nodes, width = state.shape
    tile = tiles.shape[1]
    own = nodes // tile
    dom_blocks = stale_domain.shape[0] // tile
    for b in range(own):
        extended[b] = state[b * tile : (b + 1) * tile, :]
    for b in range(dom_blocks):
        extended[own + b] = stale_domain[b * tile : (b + 1) * tile, :]
    for b in range(stale_group.shape[0] // tile):
        extended[own + dom_blocks + b] = stale_group[b * tile : (b + 1) * tile, :]
    gathered[...] = jnp.zeros_like(gathered)
    ext_grad[...] = jnp.zeros_like(ext_grad)
    rounds = count[0] // UNROLL

    def gather_tiles(i, carry):
        for u in range(UNROLL):
            k = i * UNROLL + u
            gathered[target[k]] += dot(tiles[k], extended[source[k]])
        return carry

    lax.fori_loop(0, rounds, gather_tiles, 0)
    around = gathered[...].reshape(nodes, width).astype(BF16)
    own_rows = state[...]
    preact = dot(own_rows, weight_self[...]) + dot(around, weight_neighbour[...]) + bias[...]
    sigmoid = jax.nn.sigmoid(preact)
    activation[...] = (preact * sigmoid).astype(BF16)
    slope = sigmoid * (1.0 + preact * (1.0 - sigmoid))
    pre_grad = (cotangent[...].astype(F32) * slope).astype(BF16)

    grads = jnp.concatenate(
        [
            lax.dot_general(own_rows, pre_grad, CONTRACT_FIRST, preferred_element_type=F32),
            lax.dot_general(around, pre_grad, CONTRACT_FIRST, preferred_element_type=F32),
        ],
        0,
    )
    column = jnp.sum(pre_grad.astype(F32), 0, keepdims=True)
    chunks, chunk_rows, lanes = partial.shape
    body = chunk_rows - EXTRA
    parts = width // lanes
    halves = [grads[:, h * lanes : (h + 1) * lanes].reshape(-1, body, lanes) for h in range(parts)]
    extra = jnp.concatenate(
        [column[:, h * lanes : (h + 1) * lanes] for h in range(parts)]
        + [jnp.zeros((EXTRA - parts, lanes), F32)],
        0,
    )
    partial[...] = jnp.concatenate(
        [
            jnp.concatenate(halves, 0),
            jnp.broadcast_to(extra[None], (chunks, EXTRA, lanes)),
        ],
        1,
    ).astype(BF16)

    agg[...] = (
        lax.dot_general(pre_grad, weight_neighbour[...], CONTRACT_LAST, preferred_element_type=F32)
        .astype(BF16)
        .reshape(own, tile, width)
    )

    def return_tiles(i, carry):
        for u in range(UNROLL):
            k = i * UNROLL + u
            ext_grad[source[k]] += lax.dot_general(
                tiles[k], agg[target[k]], CONTRACT_FIRST, preferred_element_type=F32
            )
        return carry

    lax.fori_loop(0, rounds, return_tiles, 0)
    own_term = lax.dot_general(
        pre_grad, weight_self[...], CONTRACT_LAST, preferred_element_type=F32
    )
    state_gradient[...] = (
        own_term + ext_grad[0:own].reshape(nodes, width) + stale_gradient[...].astype(F32)
    ).astype(BF16)

    def packed(indices, counts, back, peers):
        named = slot_matrix(indices[...], counts[...], nodes)
        rows = lax.dot_general(named, own_rows, CONTRACT_FIRST, preferred_element_type=F32)
        return jnp.concatenate(
            [rows.reshape(peers, -1, width), back.reshape(peers, -1, width)], 1
        ).astype(BF16)

    out_domain[...] = packed(
        send_domain, count_domain, ext_grad[own : own + dom_blocks], out_domain.shape[0]
    )
    out_group[...] = packed(
        send_group, count_group, ext_grad[own + dom_blocks :], out_group.shape[0]
    )


def sum_kernel(arrived, spread):
    total = jnp.sum(arrived[...].astype(F32), 0)
    spread[...] = jnp.broadcast_to(total[None], spread.shape).astype(BF16)


def total_kernel(scale, arrived, spread, grad_bias):
    total = jnp.sum(arrived[...].astype(F32), 0) * scale
    body = spread.shape[1]
    spread[...] = jnp.broadcast_to(total[None, 0:body], spread.shape).astype(BF16)
    grad_bias[...] = total[body : body + grad_bias.shape[0]]


def finish_kernel(arrived, grad_self, grad_neighbour):
    lanes = arrived.shape[2]
    rows, width = grad_self.shape
    parts = width // lanes
    per = arrived.shape[0] // parts
    for h in range(parts):
        part = arrived[h * per : (h + 1) * per].astype(F32).reshape(2 * rows, lanes)
        grad_self[:, h * lanes : (h + 1) * lanes] = part[0:rows]
        grad_neighbour[:, h * lanes : (h + 1) * lanes] = part[rows:]


def spread_kernel(
    from_domain,
    from_group,
    send_domain,
    count_domain,
    send_group,
    count_group,
    next_domain,
    next_group,
    next_gradient,
):
    nodes, width = next_gradient.shape

    def split(arrived):
        rows = arrived[...].astype(F32)
        half = rows.shape[1] // 2
        return (
            rows[:, :half].reshape(-1, width).astype(BF16),
            rows[:, half:].reshape(-1, width).astype(BF16),
        )

    inputs, grads = split(from_domain)
    next_domain[...] = inputs
    total = dot(slot_matrix(send_domain[...], count_domain[...], nodes), grads)
    inputs, grads = split(from_group)
    next_group[...] = inputs
    total += dot(slot_matrix(send_group[...], count_group[...], nodes), grads)
    next_gradient[...] = total.astype(BF16)


def struct(shape, dtype):
    return jax.ShapeDtypeStruct(shape, dtype)


def local(
    node_state,
    cotangent,
    stale_domain,
    stale_group,
    stale_gradient,
    tile_values,
    tile_source,
    tile_target,
    tile_count,
    send_domain,
    count_domain,
    send_group,
    count_group,
    weight_self,
    weight_neighbour,
    bias_vector,
):
    nodes, width = node_state.shape
    tile = tile_values.shape[1]
    own = nodes // tile
    domain_rows, group_rows = stale_domain.shape[0], stale_group.shape[0]
    blocks = own + (domain_rows + group_rows) // tile
    dom_peers, group_peers = count_domain.shape[0], count_group.shape[0]
    near = lax.axis_size("group") * lax.axis_size("x")
    far = lax.axis_size("z")
    lanes = 128
    body = 2 * width * width // (near * lanes)
    all_nodes = nodes * near * far
    lists = (
        send_domain.reshape(1, -1),
        count_domain.reshape(1, -1),
        send_group.reshape(1, -1),
        count_group.reshape(1, -1),
    )
    activation, state_gradient, out_domain, out_group, partial = pl.pallas_call(
        layer_kernel,
        out_shape=(
            struct((nodes, width), BF16),
            struct((nodes, width), BF16),
            struct((dom_peers, 2 * domain_rows // dom_peers, width), BF16),
            struct((group_peers, 2 * group_rows // group_peers, width), BF16),
            struct((near, body + EXTRA, lanes), BF16),
        ),
        in_specs=[SMEM] * 3 + [VMEM] * 13,
        out_specs=[VMEM] * 5,
        scratch_shapes=[
            pltpu.VMEM((blocks, tile, width), BF16),
            pltpu.VMEM((own, tile, width), F32),
            pltpu.VMEM((own, tile, width), BF16),
            pltpu.VMEM((blocks, tile, width), F32),
        ],
        compiler_params=kernel_params(),
        name="layer",
    )(
        tile_source,
        tile_target,
        tile_count,
        node_state,
        cotangent,
        stale_domain,
        stale_group,
        stale_gradient,
        tile_values,
        *lists,
        weight_self,
        weight_neighbour,
        bias_vector.reshape(1, -1),
    )

    arrived = lax.all_to_all(partial, ("group", "x"), 0, 0, tiled=True)
    from_domain = lax.all_to_all(out_domain, ("z", "x"), 0, 0, tiled=True)
    from_group = lax.all_to_all(out_group, "group", 0, 0, tiled=True)
    near_sum = pl.pallas_call(
        sum_kernel,
        out_shape=struct((far, body + EXTRA, lanes), BF16),
        in_specs=[VMEM],
        out_specs=VMEM,
        compiler_params=kernel_params(),
        name="near_sum",
    )(arrived)
    arrived = lax.all_to_all(near_sum, "z", 0, 0, tiled=True)
    total, grad_bias = pl.pallas_call(
        functools.partial(total_kernel, 1.0 / all_nodes),
        out_shape=(struct((near, body, lanes), BF16), struct((width // lanes, lanes), F32)),
        in_specs=[VMEM],
        out_specs=[VMEM] * 2,
        compiler_params=kernel_params(),
        name="total",
    )(arrived)
    arrived = lax.all_to_all(total, ("group", "x"), 0, 0, tiled=True)
    grad_self, grad_neighbour = pl.pallas_call(
        finish_kernel,
        out_shape=(struct((width, width), F32), struct((width, width), F32)),
        in_specs=[VMEM],
        out_specs=[VMEM] * 2,
        compiler_params=kernel_params(),
        name="finish",
    )(arrived)
    next_domain, next_group, next_gradient = pl.pallas_call(
        spread_kernel,
        out_shape=(
            struct((domain_rows, width), BF16),
            struct((group_rows, width), BF16),
            struct((nodes, width), BF16),
        ),
        in_specs=[VMEM] * 6,
        out_specs=[VMEM] * 3,
        compiler_params=kernel_params(),
        name="spread",
    )(from_domain, from_group, *lists)
    return (
        activation,
        state_gradient,
        next_domain,
        next_group,
        next_gradient,
        grad_self,
        grad_neighbour,
        grad_bias.reshape(-1),
    )


def solution(mesh):
    groups, domains = mesh.devices.shape
    x_size = X_SIZE if domains > X_SIZE else 2
    fine = Mesh(mesh.devices.reshape(groups, domains // x_size, x_size), ("group", "z", "x"))
    every = ("group", "z", "x")
    rows, vector, copied = P(every, None), P(every), P()
    return jax.shard_map(
        local,
        mesh=fine,
        in_specs=(rows,) * 5
        + (P(every, None, None),)
        + (vector,) * 7
        + (copied,) * 3,
        out_specs=(rows,) * 5 + (copied,) * 3,
        check_vma=False,
    )
```

time: 608 us -> 145 us (0.24)
  the two profiles are of different devices: /device:TPU:1 before, /device:TPU:2 now
where the time goes in v1:
time: 145 us; the launch traced here: 144 us
  blocking collectives  79 us (54%)
  waiting for transfers between devices  39 us (27%)
  starting transfers between devices  9.85 us (7%)
  local copies, waits for them, and re-layouts  8.36 us (6%)
  Pallas kernels  6.76 us (5%)
    all_to_all x1, blocking collectives, local(): arrived = lax.all_to_all(partial, ('group', 'x'), 0, 0, tiled=True)  31.7 us
    all_to_all x1, waiting for transfers between devices, local(): from_domain = lax.all_to_all(out_domain, ('z', 'x'), 0, 0, tiled=True)  30.9 us
    all_to_all x1, blocking collectives, local(): arrived = lax.all_to_all(near_sum, 'z', 0, 0, tiled=True)  28.5 us
    all_to_all x1, blocking collectives, local(): arrived = lax.all_to_all(total, ('group', 'x'), 0, 0, tiled=True)  18.8 us
    unnamed x30, local copies, waits for them, and re-layouts  8.36 us
    all_to_all x1, waiting for transfers between devices, local(): from_group = lax.all_to_all(out_group, 'group', 0, 0, tiled=True)  8.11 us
    all_to_all x1, starting transfers between devices, local(): from_domain = lax.all_to_all(out_domain, ('z', 'x'), 0, 0, tiled=True)  6.34 us
    pallas_call x1, Pallas kernels, local(): pl.pallas_call(layer_kernel, out_shape=(struct((nodes, width), BF16), str...  4.06 us
  transfers between devices with their start and end apart: 2, of which 2 were waited for; matrix products, arithmetic and copies ran while one was open for 0% of the time, Pallas kernels for 1%

profile of v1, /device:TPU:2, one launch (start us, length us, event | category | flops | bytes accessed | tf_op | source)
XLA Modules:
  0.0 144.3 jit_solution(4752977448842029992)
XLA Ops:
  1.3 0.0 copy-start.12
  1.3 0.0 copy-start.13
  1.3 0.0 copy-start.14
  1.3 0.0 copy-start.8
  1.3 0.0 copy-start.9
  1.3 0.0 copy-start.10
  1.3 0.0 copy-start.11
  1.4 0.6 copy-done.12
  2.0 0.0 copy-done.13
  2.0 0.0 copy-done.14
  2.0 0.0 copy-done.8
  2.0 0.0 copy-done.9
  2.0 0.0 copy-done.10
  2.0 0.0 copy-done.11
  2.0 0.0 copy-start
  2.0 1.2 copy-done
  3.3 0.0 copy-start.1
  3.3 0.9 copy-done.1
  4.2 0.0 copy-start.2
  4.2 0.9 copy-done.2
  5.2 0.0 copy-start.3
  5.2 0.9 copy-done.3
  6.1 0.0 copy-start.4
  6.1 0.9 copy-done.4
  7.1 0.0 copy-start.5
  7.1 0.9 copy-done.5
  8.0 0.0 copy-start.6
  8.0 0.9 copy-done.6
  8.9 0.0 copy-start.7
  8.9 0.8 copy-done.7
  9.7 4.1 %layer.1 = (bf16[512,256]{1,0:T(8,128)(2,1)}, bf16[512,256]{1,0:T(8,128)(2,1)}, bf16[64,16,256]{2,1,0:T(8,128)(2,1)}, bf16[16,16,256]{2,1,0:T(8,128)(2,1)}, bf16[64,24,128]{2,1,0:T(8,128)(2,1)S(1)}) custom-call(s32[32]{0:T(128)S(1)} %copy-done.13, s32[32]{0:T(128)S(1)} %copy-done.14, s32[1]{0:T(128)S(6)} %copy.24.count, bf16[512,256]{1,0:T(8,128)(2,1)S(1)} %copy-done.1, ...), custom_call_target="tpu_custom_call" | custom-call | tf_op jit(solution)/shard_map/layer/pallas_call | solution.py:254
  13.8 31.7 %all_to_all.25.arrived = bf16[64,24,128]{2,1,0:T(8,128)(2,1)S(1)} all-to-all(bf16[64,24,128]{2,1,0:T(8,128)(2,1)S(1)} %get-tuple-element.27), channel_id=1, replica_groups=mesh['group'=16,'z'=16,'x'=4] {'group','x'}, dimensions={0} | all-to-all | bytes 786432 | tf_op jit(solution)/shard_map/all_to_all | solution.py:289
  45.4 0.1 near_sum.1
  45.5 28.5 %all_to_all.26.arrived = bf16[16,24,128]{2,1,0:T(8,128)(2,1)S(1)} all-to-all(bf16[16,24,128]{2,1,0:T(8,128)(2,1)S(1)} %near_sum.1), channel_id=1, replica_groups=mesh['group'=16,'z'=16,'x'=4] {'z'}, dimensions={0} | all-to-all | bytes 196608 | tf_op jit(solution)/shard_map/all_to_all | solution.py:300
  74.0 3.5 %all-to-all-start.1 = ((bf16[16,16,256]{2,1,0:T(8,128)(2,1)}), bf16[16,16,256]{2,1,0:T(8,128)(2,1)S(1)}, u32[]{:S(2)}, u32[]{:S(2)}) async-start(bf16[16,16,256]{2,1,0:T(8,128)(2,1)} %get-tuple-element.23), calls=%async_computation.1 | async-start | bytes 262144 | tf_op jit(solution)/shard_map/all_to_all | solution.py:291
  77.5 0.6 total.1
  78.1 8.1 %all-to-all-done.1.from_group = bf16[16,16,256]{2,1,0:T(8,128)(2,1)S(1)} async-done(((bf16[16,16,256]{2,1,0:T(8,128)(2,1)}), bf16[16,16,256]{2,1,0:T(8,128)(2,1)S(1)}, u32[]{:S(2)}, u32[]{:S(2)}) %all-to-all-start.1) | async-done | bytes 131104 | tf_op jit(solution)/shard_map/all_to_all | solution.py:291
  86.2 18.8 %all_to_all.27.arrived = bf16[64,16,128]{2,1,0:T(8,128)(2,1)S(1)} all-to-all(bf16[64,16,128]{2,1,0:T(8,128)(2,1)S(1)} %get-tuple-element.28), channel_id=1, replica_groups=mesh['group'=16,'z'=16,'x'=4] {'group','x'}, dimensions={0} | all-to-all | bytes 524288 | tf_op jit(solution)/shard_map/all_to_all | solution.py:309
  105.0 6.3 %all-to-all-start = ((bf16[64,16,256]{2,1,0:T(8,128)(2,1)}), bf16[64,16,256]{2,1,0:T(8,128)(2,1)S(1)}, u32[]{:S(2)}, u32[]{:S(2)}) async-start(bf16[64,16,256]{2,1,0:T(8,128)(2,1)} %get-tuple-element.22), calls=%async_computation | async-start | bytes 1048576 | tf_op jit(solution)/shard_map/all_to_all | solution.py:290
  111.4 0.8 finish.1
  112.2 30.9 %all-to-all-done.from_domain = bf16[64,16,256]{2,1,0:T(8,128)(2,1)S(1)} async-done(((bf16[64,16,256]{2,1,0:T(8,128)(2,1)}), bf16[64,16,256]{2,1,0:T(8,128)(2,1)S(1)}, u32[]{:S(2)}, u32[]{:S(2)}) %all-to-all-start) | async-done | bytes 524320 | tf_op jit(solution)/shard_map/all_to_all | solution.py:290
  143.1 1.2 spread.1
Async XLA Ops:
  1.3 0.7 copy-start.12
  1.3 0.7 copy-start.13
  1.3 0.7 copy-start.14
  1.3 0.7 copy-start.8
  1.3 0.7 copy-start.9
  1.3 0.7 copy-start.10
  1.3 0.7 copy-start.11
  2.0 1.2 copy-start
  3.3 0.9 copy-start.1
  4.2 0.9 copy-start.2
  5.2 0.9 copy-start.3
  6.1 0.9 copy-start.4
  7.1 0.9 copy-start.5
  8.0 0.9 copy-start.6
  8.9 0.8 copy-start.7
  74.0 12.2 %all-to-all-start.1 = ((bf16[16,16,256]{2,1,0:T(8,128)(2,1)}), bf16[16,16,256]{2,1,0:T(8,128)(2,1)S(1)}, u32[]{:S(2)}, u32[]{:S(2)}) async-start(bf16[16,16,256]{2,1,0:T(8,128)(2,1)} %get-tuple-element.23), calls=%async_computation.1 | async-start | bytes 262144 | tf_op jit(solution)/shard_map/all_to_all | solution.py:291
  105.0 38.1 %all-to-all-start = ((bf16[64,16,256]{2,1,0:T(8,128)(2,1)}), bf16[64,16,256]{2,1,0:T(8,128)(2,1)S(1)}, u32[]{:S(2)}, u32[]{:S(2)}) async-start(bf16[64,16,256]{2,1,0:T(8,128)(2,1)} %get-tuple-element.22), calls=%async_computation | async-start | bytes 1048576 | tf_op jit(solution)/shard_map/all_to_all | solution.py:290
